TPU v7x, 1024 devices: a whole 4x4x32 slice. The times are simulated.
1024 devices in a mesh: cell: 128 (over z, y), hour: 8 (over x, core).
Axes of the slice: x: 4, y: 4, z: 32, core: 2. Of those that a mesh axis runs over, the one named last changes fastest.
Arguments:
- slab: float32 [32768, 96, 256], P('cell', 'hour'), may hold values from -520 to 520
- start: float32 [256, 64], replicated, may hold values from -4 to 4
Outputs:
- subspace: float32 [256, 64], replicated
- hour_gram: float32 [96, 96], P('hour')
All inputs are finite; a program needn't handle non-finite values.
Results may differ from a plain program's by a relative error of at most 0.0003.
Values sent between devices are 32-bit elements; how exact they have to be, the bound alone decides.
No kernel may reach another device: no remote copies, remote signals or barrier semaphores. Data moves between devices by JAX's collectives and lax.ppermute only.
A program may use at most 32 MiB of HBM per device.

v0:
```python
import jax
import jax.numpy as jnp
from jax import lax
from jax.sharding import PartitionSpec as P

POWER = 2


def orthonormalize(columns):
    for repeat in range(2):
        inner_gram = jnp.dot(
            columns.T, columns, precision=lax.Precision.HIGHEST, preferred_element_type=jnp.float32
        )
        factor_low = jnp.linalg.cholesky(inner_gram)
        columns = jax.scipy.linalg.solve_triangular(factor_low, columns.T, lower=True).T
    return columns


def local(slab, start):
    cell_count, hour_count, kpi_count = slab.shape
    keep_count = start.shape[1]
    unfolded = slab.reshape(cell_count * hour_count, kpi_count)
    partial_gram = lax.dot_general(
        unfolded,
        unfolded,
        (((0,), (0,)), ((), ())),
        precision=lax.Precision.HIGHEST,
        preferred_element_type=jnp.float32,
    )
    gram_total = lax.psum(partial_gram, ("cell", "hour"))
    all_cells = cell_count * lax.axis_size("cell")
    all_hours = hour_count * lax.axis_size("hour")
    kpi_gram = gram_total / (all_cells * all_hours)
    subspace = start
    for repeat in range(POWER):
        subspace = orthonormalize(
            jnp.dot(
                kpi_gram,
                subspace,
                precision=lax.Precision.HIGHEST,
                preferred_element_type=jnp.float32,
            )
        )
    core_slab = jnp.dot(
        unfolded, subspace, precision=lax.Precision.HIGHEST, preferred_element_type=jnp.float32
    ).reshape(cell_count, hour_count, keep_count)
    regrouped = lax.all_to_all(core_slab, "hour", split_axis=0, concat_axis=1, tiled=True)
    local_gram = jnp.einsum("chr,cgr->hg", regrouped, regrouped, precision=lax.Precision.HIGHEST)
    hour_total = lax.psum(local_gram, ("cell", "hour"))
    row_block = lax.dynamic_slice_in_dim(
        hour_total, lax.axis_index("hour") * hour_count, hour_count, 0
    )
    hour_gram = row_block / (all_cells * keep_count)
    return (subspace, hour_gram)


def solution(mesh):
    return jax.shard_map(
        local,
        mesh=mesh,
        in_specs=(P("cell", "hour", None), P()),
        out_specs=(P(), P("hour", None)),
        check_vma=False,
    )
```

profile of v0, /device:TPU:1, one launch (start us, length us, event | category | flops | bytes accessed | tf_op | source)
XLA Modules:
  0.0 1141.5 jit_solution(15532869913612634178)
XLA Ops:
  7.2 8.8 convolution_bitcast_fusion.1
  16.1 3.8 copy.15
  19.9 2.9 reshape.18
  22.8 869.5 %all-reduce.2.cloned.1.call-done = f32[256,256]{1,0:T(8,128)} async-done(((f32[256,256]{1,0:T(8,128)}), f32[256,256]{1,0:T(8,128)}) %all-reduce.2.cloned.1.call-update) | async-done | bytes 262160 | tf_op jit(solution)/shard_map/psum | solution.py:30
  892.3 1.3 fusion.7
  894.0 5.8 cholesky.74
  901.2 4.9 custom-call.8
  906.6 5.8 cholesky.85
  913.2 0.7 fusion.16
  913.8 4.9 custom-call.9
  919.0 1.3 fusion.5
  920.6 5.8 cholesky.96
  927.8 4.9 custom-call.10
  933.3 5.8 cholesky.107
  940.5 4.9 custom-call.11
  945.7 4.0 convolution_bitcast_fusion
  949.7 2.8 copy.16
  952.4 1.7 reshape.19
  954.1 1.9 reshape.22
  956.0 6.4 all-to-all-start
  962.5 12.3 %all-to-all-done = f32[8,1,24576]{2,1,0:T(1,128)S(1)} async-done(((f32[8,1,24576]{2,1,0:T(1,128)}), f32[8,1,24576]{2,1,0:T(1,128)S(1)}, u32[]{:S(2)}, u32[]{:S(2)}) %all-to-all-start) | async-done | bytes 786464 | tf_op jit(solution)/shard_map/all_to_all | solution.py:47
  975.3 2.5 reduce.4
  978.9 3.2 fusion.2
  982.1 152.0 %psum.15 = f32[96,96]{1,0:T(8,128)S(1)} all-reduce(f32[96,96]{1,0:T(8,128)S(1)} %fusion.2), channel_id=1, replica_groups=mesh['cell'=128,'hour'=8] {'cell','hour'}, use_global_device_ids=true, to_apply=%region_3.6 | all-reduce | flops 9216 | bytes 73728 | tf_op jit(solution)/shard_map/psum | solution.py:49
  (39 shorter events, 9.2 us)
Async XLA Ops:
  7.2 885.2 %copy-start = (f32[256,64]{0,1:T(8,128)S(1)}, f32[256,64]{0,1:T(8,128)}, u32[]{:S(2)}) copy-start(f32[256,64]{0,1:T(8,128)} %param.6) | copy-start | bytes 196612
  7.2 8.9 copy-start.1
  7.2 885.1 %all-reduce.2.cloned.1.call-start = ((), (), s32[]{:S(2)}) async-start(), calls=%async_computation.1 | async-start | bytes 524288 | tf_op jit(solution)/shard_map/psum | solution.py:30
  945.6 6.8 copy-start.2
  956.0 18.7 %all-to-all-start = ((f32[8,1,24576]{2,1,0:T(1,128)}), f32[8,1,24576]{2,1,0:T(1,128)S(1)}, u32[]{:S(2)}, u32[]{:S(2)}) async-start(f32[8,1,24576]{2,1,0:T(1,128)} %reshape.22), calls=%async_computation | async-start | bytes 1572864 | tf_op jit(solution)/shard_map/all_to_all | solution.py:47
Sparse Core Ops, SparseCore 0:
  16.2 876.1 all-reduce.1
where the time goes:
time: 1140 us
  waiting for transfers between devices  882 us (77%)
  blocking collectives  152 us (13%)
  other arithmetic  51.4 us (5%)
  matrix products  20.5 us (2%)
  local copies, waits for them, and re-layouts  15 us (1%)
  between operations  14.3 us (1%)
    psum x1, waiting for transfers between devices, local(): gram_total = lax.psum(partial_gram, ('cell', 'hour'))  870 us
    psum x1, blocking collectives, local(): hour_total = lax.psum(local_gram, ('cell', 'hour'))  152 us
    another operation x12, other arithmetic, orthonormalize(): factor_low = jnp.linalg.cholesky(inner_gram)  26.1 us
  transfers between devices with their start and end apart: 2, of which 2 were waited for; matrix products, arithmetic and copies ran while one was open for 1% of the time, Pallas kernels for 0%

commit v1 on v0

v1 whole, which is shorter than its diff:
```python
import functools

import jax
import jax.numpy as jnp
from jax import lax
from jax.experimental import pallas as pl
from jax.experimental.pallas import tpu as pltpu
from jax.sharding import Mesh, PartitionSpec as P

POWER = 2
F32 = jnp.float32
BF16 = jnp.bfloat16
HIGHEST = lax.Precision.HIGHEST
NEAR = ("y", "x", "core")
HOUR = ("x", "core")


def split(values):
    high = values.astype(BF16)
    low = (values - high.astype(F32)).astype(BF16)
    return high, low


def dot(a, b, contract):
    return lax.dot_general(a, b, (contract, ((), ())), preferred_element_type=F32)


def dot_full(a, b, contract):
    return lax.dot_general(
        a, b, (contract, ((), ())), precision=HIGHEST, preferred_element_type=F32
    )


def gram_kernel(scale, slab_ref, gram_ref, high_ref, low_ref):
    step = pl.program_id(0)
    cells, hours, kpis = slab_ref.shape
    block = slab_ref[...]
    upper = block[:, 0:8, :].reshape(cells * 8, kpis)
    half = cells // 2
    rest = jnp.concatenate([block[:half, 8:12, :], block[half:, 8:12, :]], axis=1)
    rows = jnp.concatenate([upper, rest.reshape(half * 8, kpis)], axis=0)
    high, low = split(rows)
    high_ref[0] = high
    low_ref[0] = low
    first = ((0,), (0,))
    cross = dot(high, low, first)
    part = dot(high, high, first) + dot(low, low, first) + (cross + cross.T)

    @pl.when(step == 0)
    def _():
        gram_ref[...] = part

    @pl.when(step > 0)
    def _():
        gram_ref[...] += part

    @pl.when(step == pl.num_programs(0) - 1)
    def _():
        gram_ref[...] = gram_ref[...] * scale


def slab_gram(slab, quarters, scale):
    cells, hours, kpis = slab.shape
    block = cells // quarters
    rows = block * hours
    return pl.pallas_call(
        functools.partial(gram_kernel, scale),
        grid=(quarters,),
        in_specs=[pl.BlockSpec((block, hours, kpis), lambda i: (i, 0, 0))],
        out_specs=[
            pl.BlockSpec((kpis, kpis), lambda i: (0, 0)),
            pl.BlockSpec((1, rows, kpis), lambda i: (i, 0, 0)),
            pl.BlockSpec((1, rows, kpis), lambda i: (i, 0, 0)),
        ],
        out_shape=[
            jax.ShapeDtypeStruct((kpis, kpis), F32),
            jax.ShapeDtypeStruct((quarters, rows, kpis), BF16),
            jax.ShapeDtypeStruct((quarters, rows, kpis), BF16),
        ],
        compiler_params=pltpu.CompilerParams(vmem_limit_bytes=40 * 2**20),
    )(slab)


def inverse_factor(gram):
    size = gram.shape[0]
    blocks = size // 8
    row_index = lax.broadcasted_iota(jnp.int32, (size, size), 0)
    column_index = lax.broadcasted_iota(jnp.int32, (size, size), 1)
    identity = jnp.where(row_index == column_index, 1.0, 0.0).astype(F32)
    whole = jnp.concatenate([gram, identity], axis=1)
    work = [whole[8 * b : 8 * b + 8, :] for b in range(blocks)]
    width = 2 * size
    sublane = lax.broadcasted_iota(jnp.int32, (8, width), 0)
    for panel in range(blocks):
        spread = {}
        for k in range(8):
            for b in range(panel, blocks):
                column = work[b][:, 8 * panel + k : 8 * panel + k + 1]
                spread[k, b] = jnp.broadcast_to(column, (8, width))
        for k in range(8):
            pivot_rows = [
                jnp.broadcast_to(spread[l, panel][k : k + 1, :], (8, width)) for l in range(k, 8)
            ]
            inverse = 1.0 / pivot_rows[0]
            pivot_work = jnp.broadcast_to(work[panel][k : k + 1, :], (8, width))
            for b in range(panel, blocks):
                factor = spread[k, b] * inverse
                if b == panel:
                    factor = jnp.where(sublane > k, factor, 0.0)
                for l in range(k + 1, 8):
                    spread[l, b] = spread[l, b] - factor * pivot_rows[l - k]
                work[b] = work[b] - factor * pivot_work
    whole = jnp.concatenate(work, axis=0)
    diagonal = jnp.sum(
        jnp.where(row_index == column_index, whole[:, :size], 0.0), axis=1, keepdims=True
    )
    return whole[:, size:] * lax.rsqrt(diagonal)


def orthonormalize(columns):
    for repeat in range(2):
        inner_gram = dot_full(columns, columns, ((0,), (0,)))
        inverse = inverse_factor(inner_gram)
        columns = dot_full(columns, inverse, ((1,), (1,)))
    return columns


def core_kernel(gram_ref, start_ref, high_ref, low_ref, subspace_ref, core_ref, high, low, sems):
    copies = [
        pltpu.make_async_copy(high_ref, high, sems.at[0]),
        pltpu.make_async_copy(low_ref, low, sems.at[1]),
    ]
    for copy in copies:
        copy.start()
    gram = gram_ref[...]
    subspace = start_ref[...]
    for repeat in range(POWER):
        subspace = orthonormalize(dot_full(gram, subspace, ((1,), (0,))))
    subspace_ref[...] = subspace
    quarters, rows, kpis = high.shape
    keep = subspace.shape[1]
    basis_high, basis_low = split(subspace)
    for copy in copies:
        copy.wait()
    plain = ((1,), (0,))

    def place(basis, q):
        parts = []
        if q:
            parts.append(jnp.zeros((kpis, keep * q), BF16))
        parts.append(basis)
        if q < quarters - 1:
            parts.append(jnp.zeros((kpis, keep * (quarters - 1 - q)), BF16))
        return jnp.concatenate(parts, axis=1)

    bases = [(place(basis_high, q), place(basis_low, q)) for q in range(quarters)]
    devices, piece, width = core_ref.shape
    group = piece // 3
    third = rows // 3
    for j in range(devices):
        for part in range(3):
            at = pl.ds(part * third + j * group, group)
            total = jnp.zeros((group, width), F32)
            for q in range(quarters):
                total += dot(high[q, at, :], bases[q][0], plain)
                total += dot(high[q, at, :], bases[q][1], plain)
                total += dot(low[q, at, :], bases[q][0], plain)
            core_ref[j, part * group : (part + 1) * group, :] = total


def subspace_and_core(gram, start, high, low, devices):
    quarters, rows, kpis = high.shape
    keep = start.shape[1]
    vmem = pl.BlockSpec(memory_space=pltpu.VMEM)
    hbm = pl.BlockSpec(memory_space=pl.ANY)
    return pl.pallas_call(
        core_kernel,
        in_specs=[vmem, vmem, hbm, hbm],
        out_specs=[vmem, vmem],
        out_shape=[
            jax.ShapeDtypeStruct((kpis, keep), F32),
            jax.ShapeDtypeStruct((devices, rows // devices, quarters * keep), F32),
        ],
        scratch_shapes=[
            pltpu.VMEM(high.shape, BF16),
            pltpu.VMEM(low.shape, BF16),
            pltpu.SemaphoreType.DMA((2,)),
        ],
        compiler_params=pltpu.CompilerParams(vmem_limit_bytes=40 * 2**20),
    )(gram, start, high, low)


def hour_kernel(hours, scale, core_ref, gram_ref):
    devices, piece, width = core_ref.shape
    group = piece // 3
    keep_first = lax.broadcasted_iota(jnp.int32, (8, width), 0) < hours - 8
    size = devices * 16
    total = jnp.zeros((size, size), F32)
    last = ((1,), (1,))
    for p in range(group // 8):
        for s in range(2):
            tiles = []
            for d in range(devices):
                tiles.append(core_ref[d, s * group + 8 * p : s * group + 8 * p + 8, :])
                rest = core_ref[d, 2 * group + 8 * p : 2 * group + 8 * p + 8, :]
                if s:
                    rest = pltpu.roll(rest, 4, 0)
                tiles.append(jnp.where(keep_first, rest, 0.0))
            high, low = split(jnp.concatenate(tiles, axis=0))
            cross = dot(high, low, last)
            total += dot(high, high, last) + dot(low, low, last) + (cross + cross.T)
    at = lax.broadcasted_iota(jnp.int32, (size, size), 0)
    to = lax.broadcasted_iota(jnp.int32, (size, size), 1)
    pick = jnp.where((at // 16) * hours + at % 16 == to, 1.0, 0.0)
    pick = jnp.where(at % 16 < hours, pick, 0.0).astype(F32)
    packed = dot_full(total, pick, ((1,), (0,))) * scale
    packed = packed.reshape(devices, 16, size)
    for copy in range(gram_ref.shape[0]):
        gram_ref[copy] = packed


def hour_gram_parts(core, hours, copies, scale):
    devices = core.shape[0]
    vmem = pl.BlockSpec(memory_space=pltpu.VMEM)
    return pl.pallas_call(
        functools.partial(hour_kernel, hours, scale),
        in_specs=[vmem],
        out_specs=vmem,
        out_shape=jax.ShapeDtypeStruct((copies, devices, 16, devices * 16), F32),
        compiler_params=pltpu.CompilerParams(vmem_limit_bytes=40 * 2**20),
    )(core)


def swap(values, axes):
    return lax.all_to_all(values, axes, 0, 0, tiled=True)


def far_sum(values):
    near_z = lax.axis_size("z_lo")
    copies = jnp.broadcast_to(values[None], (near_z,) + values.shape)
    return lax.psum(jnp.sum(swap(copies, "z_lo"), axis=0), "z_hi")


def local(slab, start):
    cell_count, hour_count, kpi_count = slab.shape
    keep_count = start.shape[1]
    hour_devices = lax.axis_size(HOUR)
    near_devices = lax.axis_size(NEAR)
    all_cells = cell_count * lax.axis_size(("z_hi", "z_lo", "y"))
    all_hours = hour_count * hour_devices
    quarters = 256 // keep_count

    partial_gram, high, low = slab_gram(slab, quarters, 1.0 / (all_cells * all_hours))
    pieces = partial_gram.reshape(near_devices, kpi_count // near_devices, kpi_count)
    piece = far_sum(jnp.sum(swap(pieces, NEAR), axis=0))
    pieces = swap(jnp.broadcast_to(piece[None], (near_devices,) + piece.shape), NEAR)
    kpi_gram = pieces.reshape(kpi_count, kpi_count)

    subspace, core = subspace_and_core(kpi_gram, start, high, low, hour_devices)
    core = swap(core, HOUR)
    y_devices = lax.axis_size("y")
    parts = hour_gram_parts(core, hour_count, y_devices, 1.0 / (all_cells * keep_count))
    parts = parts.reshape((near_devices,) + parts.shape[2:])
    rows = far_sum(jnp.sum(swap(parts, NEAR), axis=0))
    return subspace, rows[:hour_count, :all_hours]


def solution(mesh):
    fine = Mesh(
        mesh.devices.reshape(8, 4, 4, 4, 2), ("z_hi", "z_lo", "y", "x", "core")
    )
    return jax.shard_map(
        local,
        mesh=fine,
        in_specs=(P(("z_hi", "z_lo", "y"), HOUR, None), P()),
        out_specs=(P(), P(HOUR, None)),
        check_vma=False,
    )
```

time: 1140 us -> 163 us (0.14)
  the two profiles are of different devices: /device:TPU:1 before, /device:TPU:2 now
where the time goes in v1:
time: 163 us; the launch traced here: 162 us
  blocking collectives  115 us (71%)
  Pallas kernels  19.1 us (12%)
  waiting for transfers between devices  11.7 us (7%)
  starting transfers between devices  8.36 us (5%)
  local copies, waits for them, and re-layouts  7.37 us (5%)
    all_to_all x4, blocking collectives, swap(): return lax.all_to_all(values, axes, 0, 0, tiled=True)  59.7 us
    psum x2, blocking collectives, far_sum(): return lax.psum(jnp.sum(swap(copies, 'z_lo'), axis=0), 'z_hi')  55.1 us
    pallas_call x1, Pallas kernels, subspace_and_core(): pl.pallas_call(core_kernel, in_specs=[vmem, vmem, hbm, hbm], out_specs=[v...  15.8 us
    all_to_all x2, waiting for transfers between devices, swap(): return lax.all_to_all(values, axes, 0, 0, tiled=True)  11.7 us
    all_to_all x2, starting transfers between devices, swap(): return lax.all_to_all(values, axes, 0, 0, tiled=True)  8.36 us
    unnamed x7, local copies, waits for them, and re-layouts  6.06 us
  transfers between devices with their start and end apart: 2, of which 2 were waited for; matrix products, arithmetic and copies ran while one was open for 1% of the time, Pallas kernels for 0%

profile of v1, /device:TPU:2, one launch (start us, length us, event | category | flops | bytes accessed | tf_op | source)
XLA Modules:
  0.0 162.2 jit_solution(2763432552522259407)
XLA Ops:
  0.6 3.8 %copy.7.slab_ref = f32[256,12,256]{2,1,0:T(8,128)S(1)} copy(f32[256,12,256]{2,0,1:T(8,128)} %param.2) | data formatting | bytes 6291456 | tf_op args[0]
  4.4 2.5 %shard_map.41 = (f32[256,256]{1,0:T(8,128)S(1)}, bf16[4,768,256]{2,1,0:T(8,128)(2,1)S(1)}, bf16[4,768,256]{2,1,0:T(8,128)(2,1)S(1)}) custom-call(f32[256,12,256]{2,1,0:T(8,128)S(1)} %copy.7.slab_ref), custom_call_target="tpu_custom_call" | custom-call | tf_op jit(solution)/shard_map/pallas_call | solution.py:66
  6.9 23.6 %all_to_all.30 = f32[32,8,256]{2,1,0:T(8,128)S(1)} all-to-all(f32[32,8,256]{2,1,0:T(8,128)S(1)} %bitcast.6), channel_id=1, replica_groups=mesh['z_hi'=8,'z_lo'=4,'y'=4,'x'=4,'core'=2] {'y','x','core'}, dimensions={0} | all-to-all | bytes 524288 | tf_op jit(solution)/shard_map/all_to_all | solution.py:235
  30.6 8.0 %all_to_all.31 = f32[4,8,256]{2,1,0:T(8,128)S(1)} all-to-all(f32[4,8,256]{2,1,0:T(8,128)S(1)} %broadcast_in_dim.6), channel_id=1, replica_groups=mesh['z_hi'=8,'z_lo'=4,'y'=4,'x'=4,'core'=2] {'z_lo'}, dimensions={0} | all-to-all | bytes 65536 | tf_op jit(solution)/shard_map/all_to_all | solution.py:235
  38.6 31.2 %psum.14 = f32[8,256]{1,0:T(8,128)S(1)} all-reduce(f32[8,256]{1,0:T(8,128)S(1)} %reduce_sum.37), channel_id=1, replica_groups=mesh['z_hi'=8,'z_lo'=4,'y'=4,'x'=4,'core'=2] {'z_hi'}, use_global_device_ids=true, to_apply=%region_2.0 | all-reduce | flops 2048 | bytes 16384 | tf_op jit(solution)/shard_map/psum | solution.py:241
  69.8 0.7 broadcast_in_dim.7
  70.5 5.1 %all-to-all-start.2 = ((f32[32,8,256]{2,1,0:T(8,128)}), f32[32,8,256]{2,1,0:T(8,128)S(1)}, u32[]{:S(2)}, u32[]{:S(2)}) async-start(f32[32,8,256]{2,1,0:T(8,128)} %broadcast_in_dim.7), calls=%async_computation.2 | async-start | bytes 524288 | tf_op jit(solution)/shard_map/all_to_all | solution.py:235
  75.6 0.9 copy.8.start_ref
  76.5 6.8 %all-to-all-done.2 = f32[32,8,256]{2,1,0:T(8,128)S(1)} async-done(((f32[32,8,256]{2,1,0:T(8,128)}), f32[32,8,256]{2,1,0:T(8,128)S(1)}, u32[]{:S(2)}, u32[]{:S(2)}) %all-to-all-start.2) | async-done | bytes 262176 | tf_op jit(solution)/shard_map/all_to_all | solution.py:235
  83.4 15.8 %shard_map.42 = (f32[256,64]{1,0:T(8,128)S(1)}, f32[8,96,256]{2,1,0:T(8,128)S(1)}) custom-call(f32[256,256]{1,0:T(8,128)S(1)} %bitcast.4, f32[256,64]{1,0:T(8,128)S(1)} %copy.8.start_ref, bf16[4,768,256]{2,1,0:T(8,128)(2,1)S(1)} %get-tuple-element.8.high_ref, bf16[4,768,256]{2,1,0:T(8,128)(2,1)S(1)} %get-tuple-element.9.low_ref), custom_call_target="tpu_custom_call" | custom-call | tf_op jit(solution)/shard_map/pallas_call | solution.py:176
  99.2 0.0 copy-start
  99.2 0.6 copy-done
  99.9 0.0 copy-start.1
  99.9 15.8 %all_to_all.32.core_ref = f32[8,96,256]{2,1,0:T(8,128)S(1)} all-to-all(f32[8,96,256]{2,1,0:T(8,128)S(1)} %get-tuple-element.11), channel_id=1, replica_groups=mesh['z_hi'=8,'z_lo'=4,'y'=4,'x'=4,'core'=2] {'x','core'}, dimensions={0} | all-to-all | bytes 1572864 | tf_op jit(solution)/shard_map/all_to_all | solution.py:235
  115.6 0.8 shard_map.43
  116.5 12.3 %all_to_all.33 = f32[32,16,128]{2,1,0:T(8,128)S(1)} all-to-all(f32[32,16,128]{2,1,0:T(8,128)S(1)} %bitcast.5), channel_id=1, replica_groups=mesh['z_hi'=8,'z_lo'=4,'y'=4,'x'=4,'core'=2] {'y','x','core'}, dimensions={0} | all-to-all | bytes 524288 | tf_op jit(solution)/shard_map/all_to_all | solution.py:235
  128.8 0.6 broadcast_in_dim.8
  129.4 3.3 %all-to-all-start.5 = ((f32[4,16,128]{2,1,0:T(8,128)}), f32[4,16,128]{2,1,0:T(8,128)S(1)}, u32[]{:S(2)}, u32[]{:S(2)}) async-start(f32[4,16,128]{2,1,0:T(8,128)} %broadcast_in_dim.8), calls=%async_computation.5 | async-start | bytes 65536 | tf_op jit(solution)/shard_map/all_to_all | solution.py:235
  132.7 0.0 copy-done.1
  132.7 0.7 copy.9
  133.4 4.9 %all-to-all-done.5 = f32[4,16,128]{2,1,0:T(8,128)S(1)} async-done(((f32[4,16,128]{2,1,0:T(8,128)}), f32[4,16,128]{2,1,0:T(8,128)S(1)}, u32[]{:S(2)}, u32[]{:S(2)}) %all-to-all-start.5) | async-done | bytes 32800 | tf_op jit(solution)/shard_map/all_to_all | solution.py:235
  138.3 23.9 %psum.15 = f32[16,128]{1,0:T(8,128)} all-reduce(f32[16,128]{1,0:T(8,128)S(1)} %reduce_sum.39), channel_id=1, replica_groups=mesh['z_hi'=8,'z_lo'=4,'y'=4,'x'=4,'core'=2] {'z_hi'}, use_global_device_ids=true, to_apply=%region_5.0 | all-reduce | flops 2048 | bytes 16384 | tf_op jit(solution)/shard_map/psum | solution.py:241
  (5 shorter events, 0.1 us)
Async XLA Ops:
  70.5 12.9 %all-to-all-start.2 = ((f32[32,8,256]{2,1,0:T(8,128)}), f32[32,8,256]{2,1,0:T(8,128)S(1)}, u32[]{:S(2)}, u32[]{:S(2)}) async-start(f32[32,8,256]{2,1,0:T(8,128)} %broadcast_in_dim.7), calls=%async_computation.2 | async-start | bytes 524288 | tf_op jit(solution)/shard_map/all_to_all | solution.py:235
  99.2 0.6 copy-start
  99.9 32.8 %copy-start.1 = (f32[256,64]{1,0:T(8,128)S(1)}, f32[256,64]{1,0:T(8,128)}, u32[]{:S(2)}) copy-start(f32[256,64]{1,0:T(8,128)} %copy-done) | copy-start | bytes 196612
  129.4 8.9 %all-to-all-start.5 = ((f32[4,16,128]{2,1,0:T(8,128)}), f32[4,16,128]{2,1,0:T(8,128)S(1)}, u32[]{:S(2)}, u32[]{:S(2)}) async-start(f32[4,16,128]{2,1,0:T(8,128)} %broadcast_in_dim.8), calls=%async_computation.5 | async-start | bytes 65536 | tf_op jit(solution)/shard_map/all_to_all | solution.py:235

commit v2 on v1

v2 whole, which is shorter than its diff:
```python
import functools

import jax
import jax.numpy as jnp
from jax import lax
from jax.experimental import pallas as pl
from jax.experimental.pallas import tpu as pltpu
from jax.sharding import Mesh, PartitionSpec as P

POWER = 2
F32 = jnp.float32
BF16 = jnp.bfloat16
HIGHEST = lax.Precision.HIGHEST
NEAR = ("y", "x", "core")
HOUR = ("x", "core")


def split(values):
    high = values.astype(BF16)
    low = (values - high.astype(F32)).astype(BF16)
    return high, low


def dot(a, b, contract):
    return lax.dot_general(a, b, (contract, ((), ())), preferred_element_type=F32)


def dot_full(a, b, contract):
    return lax.dot_general(
        a, b, (contract, ((), ())), precision=HIGHEST, preferred_element_type=F32
    )


def gram_kernel(scale, slab_ref, gram_ref, slab, sems):
    hours, cells, kpis = slab.shape
    count = sems.shape[0]
    step = hours // count
    copies = []
    for i in range(count):
        at = pl.ds(i * step, step)
        copies.append(pltpu.make_async_copy(slab_ref.at[at], slab.at[at], sems.at[i]))
        copies[-1].start()
    first = ((0,), (0,))
    even = jnp.zeros((kpis, kpis), F32)
    cross = jnp.zeros((kpis, kpis), F32)
    for i in range(count):
        at = pl.ds(i * step, step)
        copies[i].wait()
        high, low = split(slab[at].reshape(step * cells, kpis))
        cross += dot(high, low, first)
        even += dot(high, high, first) + dot(low, low, first)
    gram_ref[...] = (even + (cross + cross.T)) * scale


def slab_gram(slab, steps, scale):
    hours, cells, kpis = slab.shape
    return pl.pallas_call(
        functools.partial(gram_kernel, scale),
        in_specs=[pl.BlockSpec(memory_space=pl.ANY)],
        out_specs=pl.BlockSpec(memory_space=pltpu.VMEM),
        out_shape=jax.ShapeDtypeStruct((kpis, kpis), F32),
        scratch_shapes=[pltpu.VMEM(slab.shape, F32), pltpu.SemaphoreType.DMA((steps,))],
        compiler_params=pltpu.CompilerParams(vmem_limit_bytes=58 * 2**20),
    )(slab)


def inverse_factor(gram):
    size = gram.shape[0]
    blocks = size // 8
    width = 2 * size
    row_index = lax.broadcasted_iota(jnp.int32, (size, size), 0)
    column_index = lax.broadcasted_iota(jnp.int32, (size, size), 1)
    identity = jnp.where(row_index == column_index, 1.0, 0.0).astype(F32)
    whole = jnp.concatenate([gram, identity], axis=1)
    work = [whole[8 * b : 8 * b + 8, :] for b in range(blocks)]
    sublane = lax.broadcasted_iota(jnp.int32, (8, width), 0)

    def fill(values):
        return jnp.broadcast_to(values, (8, width))

    def spread(panel):
        first = 8 * panel
        return {
            (k, b): fill(work[b][:, first + k : first + k + 1])
            for k in range(8)
            for b in range(panel, blocks)
        }

    now = spread(0)
    for panel in range(blocks):
        later = spread(panel + 1) if panel + 1 < blocks else {}
        for k in range(8):
            inverse = 1.0 / fill(now[k, panel][k : k + 1, :])
            pivots = {m: fill(now[m, panel][k : k + 1, :]) for m in range(k + 1, 8)}
            if later:
                next_pivots = [fill(now[k, panel + 1][m : m + 1, :]) for m in range(8)]
            row = fill(work[panel][k : k + 1, :])
            for b in range(panel, blocks):
                factor = now[k, b] * inverse
                if b == panel:
                    factor = jnp.where(sublane > k, factor, 0.0)
                for m in range(k + 1, 8):
                    now[m, b] = now[m, b] - factor * pivots[m]
                if b > panel:
                    for m in range(8):
                        later[m, b] = later[m, b] - factor * next_pivots[m]
                work[b] = work[b] - factor * row
        now = later
    whole = jnp.concatenate(work, axis=0)
    diagonal = jnp.sum(
        jnp.where(row_index == column_index, whole[:, :size], 0.0), axis=1, keepdims=True
    )
    return whole[:, size:] * lax.rsqrt(diagonal)


def near_inverse_factor(gram):
    size = gram.shape[0]
    row_index = lax.broadcasted_iota(jnp.int32, (size, size), 0)
    column_index = lax.broadcasted_iota(jnp.int32, (size, size), 1)
    identity = jnp.where(row_index == column_index, 1.0, 0.0).astype(F32)
    weight = jnp.where(row_index > column_index, 1.0, 0.0).astype(F32) + 0.5 * identity
    apart = gram - identity

    def series(_):
        once = (weight * apart).astype(BF16)
        twice = weight * (apart - dot(once, once, ((1,), (1,))))
        rounded = twice.astype(BF16)
        return identity - twice + dot(rounded, rounded, ((1,), (0,)))

    return lax.cond(
        jnp.sum(apart * apart) < 2.5e-5, series, lambda _: inverse_factor(gram), 0
    )


def orthonormalize(columns):
    for factor in (inverse_factor, near_inverse_factor):
        inner_gram = dot_full(columns, columns, ((0,), (0,)))
        columns = dot_full(columns, factor(inner_gram), ((1,), (1,)))
    return columns


def core_kernel(gram_ref, start_ref, slab_ref, subspace_ref, core_ref):
    gram = gram_ref[...]
    subspace = start_ref[...].T
    for repeat in range(POWER):
        subspace = orthonormalize(dot_full(gram, subspace, ((1,), (0,))))
    subspace_ref[...] = subspace.T
    hours, cells, kpis = slab_ref.shape
    keep = subspace.shape[1]
    devices, _, group, width = core_ref.shape
    quarters = width // keep
    quarter = cells // quarters
    basis_high, basis_low = split(subspace)
    plain = ((1,), (0,))

    def place(basis, q):
        parts = []
        if q:
            parts.append(jnp.zeros((kpis, keep * q), BF16))
        parts.append(basis)
        if q < quarters - 1:
            parts.append(jnp.zeros((kpis, keep * (quarters - 1 - q)), BF16))
        return jnp.concatenate(parts, axis=1)

    bases = [(place(basis_high, q), place(basis_low, q)) for q in range(quarters)]
    batch = 4
    for h in range(0, hours, batch):
        total = jnp.zeros((batch * quarter, width), F32)
        for q in range(quarters):
            at = pl.ds(q * quarter, quarter)
            top, rest = split(slab_ref[h : h + batch, at, :].reshape(batch * quarter, kpis))
            total += dot(top, bases[q][0], plain)
            total += dot(top, bases[q][1], plain)
            total += dot(rest, bases[q][0], plain)
        for i in range(batch):
            for j in range(devices):
                at = i * quarter + j * group
                core_ref[j, h + i] = total[at : at + group]


def subspace_and_core(gram, start, slab, devices):
    hours, cells, kpis = slab.shape
    keep = start.shape[0]
    width = 256
    group = cells * keep // width // devices
    vmem = pl.BlockSpec(memory_space=pltpu.VMEM)
    return pl.pallas_call(
        core_kernel,
        in_specs=[vmem] * 3,
        out_specs=[vmem, vmem],
        out_shape=[
            jax.ShapeDtypeStruct((keep, kpis), F32),
            jax.ShapeDtypeStruct((devices, hours, group, width), F32),
        ],
        compiler_params=pltpu.CompilerParams(vmem_limit_bytes=40 * 2**20),
    )(gram, start, slab)


def hour_kernel(hours, scale, core_ref, gram_ref, halves):
    group = 8
    rows, width = core_ref.shape
    lanes = halves.shape[2]
    for part in range(width // lanes):
        halves[part] = core_ref[:, part * lanes : (part + 1) * lanes]
    all_hours = rows // group
    devices = all_hours // hours
    total = jnp.zeros((all_hours, all_hours), F32)
    last = ((1,), (1,))
    for i in range(group):
        parts = [
            halves[part, pl.ds(i, all_hours, stride=group), :] for part in range(width // lanes)
        ]
        high, low = split(jnp.concatenate(parts, axis=1))
        cross = dot(high, low, last)
        total += dot(high, high, last) + dot(low, low, last) + (cross + cross.T)
    total = total * scale
    for d in range(devices):
        block = total[d * hours : (d + 1) * hours, :]
        for copy in range(gram_ref.shape[0] // devices):
            gram_ref[copy * devices + d] = block


def hour_gram_parts(core, hours, copies, scale):
    group, width = core.shape[2:]
    all_hours = core.shape[0] * core.shape[1]
    vmem = pl.BlockSpec(memory_space=pltpu.VMEM)
    return pl.pallas_call(
        functools.partial(hour_kernel, hours, scale),
        in_specs=[vmem],
        out_specs=vmem,
        out_shape=jax.ShapeDtypeStruct((copies * core.shape[0], hours, all_hours), F32),
        scratch_shapes=[pltpu.VMEM((width // 128, all_hours * group, 128), F32)],
        compiler_params=pltpu.CompilerParams(vmem_limit_bytes=40 * 2**20),
    )(core.reshape(all_hours * group, width))


def swap(values, axes):
    return lax.all_to_all(values, axes, 0, 0, tiled=True)


def far_sum(values):
    return lax.psum(lax.optimization_barrier(lax.psum(values, "z_lo")), "z_hi")


def local(slab, start):
    cell_count, hour_count, kpi_count = slab.shape
    keep_count = start.shape[1]
    hour_devices = lax.axis_size(HOUR)
    near_devices = lax.axis_size(NEAR)
    all_cells = cell_count * lax.axis_size(("z_hi", "z_lo", "y"))
    all_hours = hour_count * hour_devices
    y_devices = lax.axis_size("y")

    slab = jnp.transpose(slab, (1, 0, 2))
    partial_gram = slab_gram(slab, 2, 1.0 / (all_cells * all_hours))
    pieces = partial_gram.reshape(near_devices, kpi_count // near_devices, kpi_count)
    piece = far_sum(jnp.sum(swap(pieces, NEAR), axis=0))
    pieces = swap(jnp.broadcast_to(piece[None], (near_devices,) + piece.shape), NEAR)
    kpi_gram = pieces.reshape(kpi_count, kpi_count)

    subspace, core = subspace_and_core(kpi_gram, start.T, slab, hour_devices)
    core = swap(core, HOUR)
    parts = hour_gram_parts(core, hour_count, y_devices, 1.0 / (all_cells * keep_count))
    hour_gram = far_sum(jnp.sum(swap(parts, NEAR), axis=0))
    return subspace.T, hour_gram


def solution(mesh):
    fine = Mesh(
        mesh.devices.reshape(8, 4, 4, 4, 2), ("z_hi", "z_lo", "y", "x", "core")
    )
    return jax.shard_map(
        local,
        mesh=fine,
        in_specs=(P(("z_hi", "z_lo", "y"), HOUR, None), P()),
        out_specs=(P(), P(HOUR, None)),
        check_vma=False,
    )
```

time: 163 us -> 154 us (0.945)
  the two profiles are of different devices: /device:TPU:2 before, /device:TPU:32 now
where the time goes in v2:
time: 154 us; the launch traced here: 153 us
  blocking collectives  139 us (90%)
  Pallas kernels  13.8 us (9%)
    psum x4, blocking collectives, far_sum(): return lax.psum(lax.optimization_barrier(lax.psum(values, 'z_lo')), 'z_hi')  82 us
    all_to_all x4, blocking collectives, swap(): return lax.all_to_all(values, axes, 0, 0, tiled=True)  56.7 us
    pallas_call x1, Pallas kernels, subspace_and_core(): pl.pallas_call(core_kernel, in_specs=[vmem] * 3, out_specs=[vmem, vmem],...  9.12 us
    pallas_call x1, Pallas kernels, slab_gram(): pl.pallas_call(functools.partial(gram_kernel, scale), in_specs=[pl.BlockS...  4.03 us

profile of v2, /device:TPU:32, one launch (start us, length us, event | category | flops | bytes accessed | tf_op | source)
XLA Modules:
  0.0 153.2 jit_solution(16324475988488158412)
XLA Ops:
  0.6 0.0 copy-start
  0.6 0.0 copy-start.1
  0.6 4.0 %shard_map.41 = f32[256,256]{1,0:T(8,128)} custom-call(f32[12,256,256]{2,1,0:T(8,128)} %bitcast.6), custom_call_target="tpu_custom_call" | custom-call | tf_op jit(solution)/shard_map/pallas_call | solution.py:57
  4.7 16.2 %all_to_all.20 = f32[32,8,256]{2,1,0:T(8,128)S(1)} all-to-all(f32[32,8,256]{2,1,0:T(8,128)} %bitcast.11), channel_id=1, replica_groups=mesh['z_hi'=8,'z_lo'=4,'y'=4,'x'=4,'core'=2] {'y','x','core'}, dimensions={0} | all-to-all | bytes 524288 | tf_op jit(solution)/shard_map/all_to_all | solution.py:238
  21.0 17.7 %psum.28 = f32[8,256]{1,0:T(8,128)S(1)} all-reduce(f32[8,256]{1,0:T(8,128)S(1)} %reduce_sum.18), channel_id=1, replica_groups=mesh['z_hi'=8,'z_lo'=4,'y'=4,'x'=4,'core'=2] {'z_lo'}, use_global_device_ids=true, to_apply=%region_1.0 | all-reduce | flops 2048 | bytes 16384 | tf_op jit(solution)/shard_map/psum | solution.py:242
  38.7 29.9 %psum.29 = f32[8,256]{1,0:T(8,128)S(1)} all-reduce(f32[8,256]{1,0:T(8,128)S(1)} %psum.28), channel_id=1, replica_groups=mesh['z_hi'=8,'z_lo'=4,'y'=4,'x'=4,'core'=2] {'z_hi'}, use_global_device_ids=true, to_apply=%region_2.0 | all-reduce | flops 2048 | bytes 16384 | tf_op jit(solution)/shard_map/psum | solution.py:242
  68.6 12.5 %all_to_all.21 = f32[32,8,256]{2,1,0:T(8,128)S(1)} all-to-all(f32[32,8,256]{2,1,0:T(8,128)S(1)} %broadcast_in_dim.2), channel_id=1, replica_groups=mesh['z_hi'=8,'z_lo'=4,'y'=4,'x'=4,'core'=2] {'y','x','core'}, dimensions={0} | all-to-all | bytes 524288 | tf_op jit(solution)/shard_map/all_to_all | solution.py:238
  81.1 0.0 copy-done
  81.1 0.0 copy-done.1
  81.1 9.1 %shard_map.42 = (f32[64,256]{1,0:T(8,128)}, f32[8,12,8,256]{3,2,1,0:T(8,128)S(1)}) custom-call(f32[256,256]{1,0:T(8,128)S(1)} %bitcast.9, f32[64,256]{1,0:T(8,128)S(1)} %bitcast.10, f32[12,256,256]{2,1,0:T(8,128)S(1)} %bitcast.7), custom_call_target="tpu_custom_call" | custom-call | tf_op jit(solution)/shard_map/pallas_call | solution.py:187
  90.2 15.6 %all_to_all.22 = f32[8,12,8,256]{3,2,1,0:T(8,128)S(1)} all-to-all(f32[8,12,8,256]{3,2,1,0:T(8,128)S(1)} %get-tuple-element.5), channel_id=1, replica_groups=mesh['z_hi'=8,'z_lo'=4,'y'=4,'x'=4,'core'=2] {'x','core'}, dimensions={0} | all-to-all | bytes 1572864 | tf_op jit(solution)/shard_map/all_to_all | solution.py:238
  105.9 0.6 shard_map.43
  106.5 12.3 %all_to_all.23 = f32[32,12,96]{2,1,0:T(8,128)S(1)} all-to-all(f32[32,12,96]{2,1,0:T(8,128)S(1)} %shard_map.43), channel_id=1, replica_groups=mesh['z_hi'=8,'z_lo'=4,'y'=4,'x'=4,'core'=2] {'y','x','core'}, dimensions={0} | all-to-all | bytes 294912 | tf_op jit(solution)/shard_map/all_to_all | solution.py:238
  118.8 10.6 %psum.30 = f32[12,96]{1,0:T(8,128)S(1)} all-reduce(f32[12,96]{1,0:T(8,128)S(1)} %reduce_sum.19), channel_id=1, replica_groups=mesh['z_hi'=8,'z_lo'=4,'y'=4,'x'=4,'core'=2] {'z_lo'}, use_global_device_ids=true, to_apply=%region_4.0 | all-reduce | flops 1152 | bytes 9216 | tf_op jit(solution)/shard_map/psum | solution.py:242
  129.4 23.8 %psum.31 = f32[12,96]{1,0:T(8,128)} all-reduce(f32[12,96]{1,0:T(8,128)S(1)} %psum.30), channel_id=1, replica_groups=mesh['z_hi'=8,'z_lo'=4,'y'=4,'x'=4,'core'=2] {'z_hi'}, use_global_device_ids=true, to_apply=%region_5.0 | all-reduce | flops 1152 | bytes 9216 | tf_op jit(solution)/shard_map/psum | solution.py:242
  (3 shorter events, 0.1 us)
Async XLA Ops:
  0.6 80.5 %copy-start = (f32[256,12,256]{2,0,1:T(8,128)S(1)}, f32[256,12,256]{2,0,1:T(8,128)}, u32[]{:S(2)}) copy-start(f32[256,12,256]{2,0,1:T(8,128)} %param.2) | copy-start | bytes 9437188
  0.6 80.5 %copy-start.1 = (f32[256,64]{0,1:T(8,128)S(1)}, f32[256,64]{0,1:T(8,128)}, u32[]{:S(2)}) copy-start(f32[256,64]{0,1:T(8,128)} %param.3) | copy-start | bytes 196612

commit v3 on v2

--- a/solution.py
+++ b/solution.py
@@ -139,18 +139,21 @@
     return columns
 
 
-def core_kernel(gram_ref, start_ref, slab_ref, subspace_ref, core_ref):
+def core_kernel(gram_ref, start_ref, slab_ref, subspace_ref, core_ref, slab, sem):
+    copy = pltpu.make_async_copy(slab_ref, slab, sem)
+    copy.start()
     gram = gram_ref[...]
     subspace = start_ref[...].T
     for repeat in range(POWER):
         subspace = orthonormalize(dot_full(gram, subspace, ((1,), (0,))))
     subspace_ref[...] = subspace.T
-    hours, cells, kpis = slab_ref.shape
+    hours, cells, kpis = slab.shape
     keep = subspace.shape[1]
     devices, _, group, width = core_ref.shape
     quarters = width // keep
     quarter = cells // quarters
     basis_high, basis_low = split(subspace)
+    copy.wait()
     plain = ((1,), (0,))
 
     def place(basis, q):
@@ -168,7 +171,7 @@
         total = jnp.zeros((batch * quarter, width), F32)
         for q in range(quarters):
             at = pl.ds(q * quarter, quarter)
-            top, rest = split(slab_ref[h : h + batch, at, :].reshape(batch * quarter, kpis))
+            top, rest = split(slab[h : h + batch, at, :].reshape(batch * quarter, kpis))
             total += dot(top, bases[q][0], plain)
             total += dot(top, bases[q][1], plain)
             total += dot(rest, bases[q][0], plain)
@@ -186,13 +189,14 @@
     vmem = pl.BlockSpec(memory_space=pltpu.VMEM)
     return pl.pallas_call(
         core_kernel,
-        in_specs=[vmem] * 3,
+        in_specs=[vmem, vmem, pl.BlockSpec(memory_space=pl.ANY)],
         out_specs=[vmem, vmem],
         out_shape=[
             jax.ShapeDtypeStruct((keep, kpis), F32),
             jax.ShapeDtypeStruct((devices, hours, group, width), F32),
         ],
-        compiler_params=pltpu.CompilerParams(vmem_limit_bytes=40 * 2**20),
+        scratch_shapes=[pltpu.VMEM(slab.shape, F32), pltpu.SemaphoreType.DMA],
+        compiler_params=pltpu.CompilerParams(vmem_limit_bytes=56 * 2**20),
     )(gram, start, slab)
 
 
@@ -215,12 +219,10 @@
         total += dot(high, high, last) + dot(low, low, last) + (cross + cross.T)
     total = total * scale
     for d in range(devices):
-        block = total[d * hours : (d + 1) * hours, :]
-        for copy in range(gram_ref.shape[0] // devices):
-            gram_ref[copy * devices + d] = block
-
-
-def hour_gram_parts(core, hours, copies, scale):
+        gram_ref[d] = total[d * hours : (d + 1) * hours, :]
+
+
+def hour_gram_parts(core, hours, scale):
     group, width = core.shape[2:]
     all_hours = core.shape[0] * core.shape[1]
     vmem = pl.BlockSpec(memory_space=pltpu.VMEM)
@@ -228,7 +230,7 @@
         functools.partial(hour_kernel, hours, scale),
         in_specs=[vmem],
         out_specs=vmem,
-        out_shape=jax.ShapeDtypeStruct((copies * core.shape[0], hours, all_hours), F32),
+        out_shape=jax.ShapeDtypeStruct((core.shape[0], hours, all_hours), F32),
         scratch_shapes=[pltpu.VMEM((width // 128, all_hours * group, 128), F32)],
         compiler_params=pltpu.CompilerParams(vmem_limit_bytes=40 * 2**20),
     )(core.reshape(all_hours * group, width))
@@ -238,8 +240,9 @@
     return lax.all_to_all(values, axes, 0, 0, tiled=True)
 
 
-def far_sum(values):
-    return lax.psum(lax.optimization_barrier(lax.psum(values, "z_lo")), "z_hi")
+def spread_out(values, axes):
+    count = lax.axis_size(axes)
+    return swap(jnp.broadcast_to(values[None], (count,) + values.shape), axes)
 
 
 def local(slab, start):
@@ -249,19 +252,20 @@
     near_devices = lax.axis_size(NEAR)
     all_cells = cell_count * lax.axis_size(("z_hi", "z_lo", "y"))
     all_hours = hour_count * hour_devices
-    y_devices = lax.axis_size("y")
 
     slab = jnp.transpose(slab, (1, 0, 2))
     partial_gram = slab_gram(slab, 2, 1.0 / (all_cells * all_hours))
     pieces = partial_gram.reshape(near_devices, kpi_count // near_devices, kpi_count)
-    piece = far_sum(jnp.sum(swap(pieces, NEAR), axis=0))
-    pieces = swap(jnp.broadcast_to(piece[None], (near_devices,) + piece.shape), NEAR)
-    kpi_gram = pieces.reshape(kpi_count, kpi_count)
+    piece = lax.psum(jnp.sum(swap(pieces, NEAR), axis=0), "z_lo")
+    piece = lax.psum(lax.optimization_barrier(piece), "z_hi")
+    kpi_gram = spread_out(piece, NEAR).reshape(kpi_count, kpi_count)
 
     subspace, core = subspace_and_core(kpi_gram, start.T, slab, hour_devices)
     core = swap(core, HOUR)
-    parts = hour_gram_parts(core, hour_count, y_devices, 1.0 / (all_cells * keep_count))
-    hour_gram = far_sum(jnp.sum(swap(parts, NEAR), axis=0))
+    parts = hour_gram_parts(core, hour_count, 1.0 / (all_cells * keep_count))
+    rows = jnp.sum(swap(parts, HOUR), axis=0)
+    rows = jnp.sum(spread_out(rows, ("z_lo", "y")), axis=0)
+    hour_gram = lax.psum(rows, "z_hi")
     return subspace.T, hour_gram
 
 

time: 154 us -> 154 us (level)
  the two profiles are of different devices: /device:TPU:32 before, /device:TPU:8 now
where the time goes in v3:
time: 154 us
  blocking collectives  138 us (90%)
  Pallas kernels  14.9 us (10%)
    all_to_all x5, blocking collectives, swap(): return lax.all_to_all(values, axes, 0, 0, tiled=True)  73.4 us
    psum x1, blocking collectives, local(): piece = lax.psum(lax.optimization_barrier(piece), 'z_hi')  31.8 us
    psum x1, blocking collectives, local(): hour_gram = lax.psum(rows, 'z_hi')  24.4 us
    pallas_call x1, Pallas kernels, subspace_and_core(): pl.pallas_call(core_kernel, in_specs=[vmem, vmem, pl.BlockSpec(memory_spa...  10.5 us
    psum x1, blocking collectives, local(): piece = lax.psum(jnp.sum(swap(pieces, NEAR), axis=0), 'z_lo')  8.55 us
    pallas_call x1, Pallas kernels, slab_gram(): pl.pallas_call(functools.partial(gram_kernel, scale), in_specs=[pl.BlockS...  3.77 us

profile of v3, /device:TPU:8, one launch (start us, length us, event | category | flops | bytes accessed | tf_op | source)
XLA Modules:
  0.0 153.8 jit_solution(4612488679575540093)
XLA Ops:
  0.6 3.8 %shard_map.41 = f32[256,256]{1,0:T(8,128)} custom-call(f32[12,256,256]{2,1,0:T(8,128)} %bitcast.7), custom_call_target="tpu_custom_call" | custom-call | tf_op jit(solution)/shard_map/pallas_call | solution.py:57
  4.4 24.2 %all_to_all.25 = f32[32,8,256]{2,1,0:T(8,128)S(1)} all-to-all(f32[32,8,256]{2,1,0:T(8,128)} %bitcast.10), channel_id=1, replica_groups=mesh['z_hi'=8,'z_lo'=4,'y'=4,'x'=4,'core'=2] {'y','x','core'}, dimensions={0} | all-to-all | bytes 524288 | tf_op jit(solution)/shard_map/all_to_all | solution.py:240
  28.6 8.5 %psum.21 = f32[8,256]{1,0:T(8,128)S(1)} all-reduce(f32[8,256]{1,0:T(8,128)S(1)} %reduce_sum.27), channel_id=1, replica_groups=mesh['z_hi'=8,'z_lo'=4,'y'=4,'x'=4,'core'=2] {'z_lo'}, use_global_device_ids=true, to_apply=%region_1.0 | all-reduce | flops 2048 | bytes 16384 | tf_op jit(solution)/shard_map/psum | solution.py:259
  37.2 31.8 %psum.22 = f32[8,256]{1,0:T(8,128)S(1)} all-reduce(f32[8,256]{1,0:T(8,128)S(1)} %psum.21), channel_id=1, replica_groups=mesh['z_hi'=8,'z_lo'=4,'y'=4,'x'=4,'core'=2] {'z_hi'}, use_global_device_ids=true, to_apply=%region_2.0 | all-reduce | flops 2048 | bytes 16384 | tf_op jit(solution)/shard_map/psum | solution.py:260
  69.0 12.7 %all_to_all.26 = f32[32,8,256]{2,1,0:T(8,128)} all-to-all(f32[32,8,256]{2,1,0:T(8,128)S(1)} %broadcast_in_dim.4), channel_id=1, replica_groups=mesh['z_hi'=8,'z_lo'=4,'y'=4,'x'=4,'core'=2] {'y','x','core'}, dimensions={0} | all-to-all | bytes 524288 | tf_op jit(solution)/shard_map/all_to_all | solution.py:240
  81.7 10.5 %shard_map.42 = (f32[64,256]{1,0:T(8,128)}, f32[8,12,8,256]{3,2,1,0:T(8,128)}) custom-call(f32[256,256]{1,0:T(8,128)} %bitcast.9, f32[64,256]{1,0:T(8,128)} %bitcast.11, f32[12,256,256]{2,1,0:T(8,128)} %bitcast.8), custom_call_target="tpu_custom_call" | custom-call | tf_op jit(solution)/shard_map/pallas_call | solution.py:190
  92.3 16.7 %all_to_all.27 = f32[8,12,8,256]{3,2,1,0:T(8,128)S(1)} all-to-all(f32[8,12,8,256]{3,2,1,0:T(8,128)} %get-tuple-element.5), channel_id=1, replica_groups=mesh['z_hi'=8,'z_lo'=4,'y'=4,'x'=4,'core'=2] {'x','core'}, dimensions={0} | all-to-all | bytes 1572864 | tf_op jit(solution)/shard_map/all_to_all | solution.py:240
  109.0 0.6 shard_map.43
  109.6 8.0 %all_to_all.28 = f32[8,12,96]{2,1,0:T(8,128)S(1)} all-to-all(f32[8,12,96]{2,1,0:T(8,128)S(1)} %shard_map.43), channel_id=1, replica_groups=mesh['z_hi'=8,'z_lo'=4,'y'=4,'x'=4,'core'=2] {'x','core'}, dimensions={0} | all-to-all | bytes 73728 | tf_op jit(solution)/shard_map/all_to_all | solution.py:240
  117.6 11.7 %all_to_all.29 = f32[16,12,96]{2,1,0:T(8,128)S(1)} all-to-all(f32[16,12,96]{2,1,0:T(8,128)S(1)} %broadcast_in_dim.5), channel_id=1, replica_groups=mesh['z_hi'=8,'z_lo'=4,'y'=4,'x'=4,'core'=2] {'z_lo','y'}, dimensions={0} | all-to-all | bytes 147456 | tf_op jit(solution)/shard_map/all_to_all | solution.py:240
  129.4 24.4 %psum.23 = f32[12,96]{1,0:T(8,128)} all-reduce(f32[12,96]{1,0:T(8,128)S(1)} %reduce_sum.29), channel_id=1, replica_groups=mesh['z_hi'=8,'z_lo'=4,'y'=4,'x'=4,'core'=2] {'z_hi'}, use_global_device_ids=true, to_apply=%region_5.0 | all-reduce | flops 1152 | bytes 9216 | tf_op jit(solution)/shard_map/psum | solution.py:268
  (5 shorter events, 0.1 us)

commit v4 on v3

--- a/solution.py
+++ b/solution.py
@@ -57,9 +57,9 @@
     return pl.pallas_call(
         functools.partial(gram_kernel, scale),
         in_specs=[pl.BlockSpec(memory_space=pl.ANY)],
-        out_specs=pl.BlockSpec(memory_space=pltpu.VMEM),
-        out_shape=jax.ShapeDtypeStruct((kpis, kpis), F32),
-        scratch_shapes=[pltpu.VMEM(slab.shape, F32), pltpu.SemaphoreType.DMA((steps,))],
+        out_specs=[pl.BlockSpec(memory_space=pltpu.VMEM)] * 2,
+        out_shape=[pltpu.VMEM((kpis, kpis), F32), pltpu.VMEM(slab.shape, F32)],
+        scratch_shapes=[pltpu.SemaphoreType.DMA((steps,))],
         compiler_params=pltpu.CompilerParams(vmem_limit_bytes=58 * 2**20),
     )(slab)
 
@@ -139,21 +139,18 @@
     return columns
 
 
-def core_kernel(gram_ref, start_ref, slab_ref, subspace_ref, core_ref, slab, sem):
-    copy = pltpu.make_async_copy(slab_ref, slab, sem)
-    copy.start()
+def core_kernel(gram_ref, start_ref, slab_ref, subspace_ref, core_ref):
     gram = gram_ref[...]
     subspace = start_ref[...].T
     for repeat in range(POWER):
         subspace = orthonormalize(dot_full(gram, subspace, ((1,), (0,))))
     subspace_ref[...] = subspace.T
-    hours, cells, kpis = slab.shape
+    hours, cells, kpis = slab_ref.shape
     keep = subspace.shape[1]
     devices, _, group, width = core_ref.shape
     quarters = width // keep
     quarter = cells // quarters
     basis_high, basis_low = split(subspace)
-    copy.wait()
     plain = ((1,), (0,))
 
     def place(basis, q):
@@ -171,7 +168,7 @@
         total = jnp.zeros((batch * quarter, width), F32)
         for q in range(quarters):
             at = pl.ds(q * quarter, quarter)
-            top, rest = split(slab[h : h + batch, at, :].reshape(batch * quarter, kpis))
+            top, rest = split(slab_ref[h : h + batch, at, :].reshape(batch * quarter, kpis))
             total += dot(top, bases[q][0], plain)
             total += dot(top, bases[q][1], plain)
             total += dot(rest, bases[q][0], plain)
@@ -189,14 +186,13 @@
     vmem = pl.BlockSpec(memory_space=pltpu.VMEM)
     return pl.pallas_call(
         core_kernel,
-        in_specs=[vmem, vmem, pl.BlockSpec(memory_space=pl.ANY)],
+        in_specs=[vmem] * 3,
         out_specs=[vmem, vmem],
         out_shape=[
             jax.ShapeDtypeStruct((keep, kpis), F32),
-            jax.ShapeDtypeStruct((devices, hours, group, width), F32),
+            pltpu.VMEM((devices, hours, group, width), F32),
         ],
-        scratch_shapes=[pltpu.VMEM(slab.shape, F32), pltpu.SemaphoreType.DMA],
-        compiler_params=pltpu.CompilerParams(vmem_limit_bytes=56 * 2**20),
+        compiler_params=pltpu.CompilerParams(vmem_limit_bytes=40 * 2**20),
     )(gram, start, slab)
 
 
@@ -254,7 +250,7 @@
     all_hours = hour_count * hour_devices
 
     slab = jnp.transpose(slab, (1, 0, 2))
-    partial_gram = slab_gram(slab, 2, 1.0 / (all_cells * all_hours))
+    partial_gram, slab = slab_gram(slab, 2, 1.0 / (all_cells * all_hours))
     pieces = partial_gram.reshape(near_devices, kpi_count // near_devices, kpi_count)
     piece = lax.psum(jnp.sum(swap(pieces, NEAR), axis=0), "z_lo")
     piece = lax.psum(lax.optimization_barrier(piece), "z_hi")

time: 154 us -> 150 us (0.974)
  Pallas kernels: 14.9 us -> 12.9 us
  blocking collectives: 138 us -> 136 us
    all_to_all x5, blocking collectives: 73.4 us -> 71.2 us  [swap(): return lax.all_to_all(values, axes, 0, 0, tiled=True)]
where the time goes in v4:
time: 150 us
  blocking collectives  136 us (91%)
  Pallas kernels  12.9 us (9%)
    all_to_all x5, blocking collectives, swap(): return lax.all_to_all(values, axes, 0, 0, tiled=True)  71.2 us
    psum x1, blocking collectives, local(): piece = lax.psum(lax.optimization_barrier(piece), 'z_hi')  32.5 us
    psum x1, blocking collectives, local(): hour_gram = lax.psum(rows, 'z_hi')  24 us
    pallas_call x1, Pallas kernels, subspace_and_core(): pl.pallas_call(core_kernel, in_specs=[vmem] * 3, out_specs=[vmem, vmem],...  9.12 us
    psum x1, blocking collectives, local(): piece = lax.psum(jnp.sum(swap(pieces, NEAR), axis=0), 'z_lo')  8.55 us
    pallas_call x1, Pallas kernels, slab_gram(): pl.pallas_call(functools.partial(gram_kernel, scale), in_specs=[pl.BlockS...  3.11 us

profile of v4, /device:TPU:8, one launch (start us, length us, event | category | flops | bytes accessed | tf_op | source)
XLA Modules:
  0.0 150.0 jit_solution(2768789069785885644)
XLA Ops:
  0.6 0.0 copy-start
  0.6 3.1 %shard_map.41 = (f32[256,256]{1,0:T(8,128)S(1)}, f32[12,256,256]{2,1,0:T(8,128)S(1)}) custom-call(f32[12,256,256]{2,1,0:T(8,128)} %bitcast.10), custom_call_target="tpu_custom_call" | custom-call | tf_op jit(solution)/shard_map/pallas_call | solution.py:57
  3.8 23.3 %all_to_all.25 = f32[32,8,256]{2,1,0:T(8,128)S(1)} all-to-all(f32[32,8,256]{2,1,0:T(8,128)S(1)} %bitcast.8), channel_id=1, replica_groups=mesh['z_hi'=8,'z_lo'=4,'y'=4,'x'=4,'core'=2] {'y','x','core'}, dimensions={0} | all-to-all | bytes 524288 | tf_op jit(solution)/shard_map/all_to_all | solution.py:236
  27.1 8.5 %psum.21 = f32[8,256]{1,0:T(8,128)S(1)} all-reduce(f32[8,256]{1,0:T(8,128)S(1)} %reduce_sum.27), channel_id=1, replica_groups=mesh['z_hi'=8,'z_lo'=4,'y'=4,'x'=4,'core'=2] {'z_lo'}, use_global_device_ids=true, to_apply=%region_1.0 | all-reduce | flops 2048 | bytes 16384 | tf_op jit(solution)/shard_map/psum | solution.py:255
  35.7 32.5 %psum.22 = f32[8,256]{1,0:T(8,128)S(1)} all-reduce(f32[8,256]{1,0:T(8,128)S(1)} %psum.21), channel_id=1, replica_groups=mesh['z_hi'=8,'z_lo'=4,'y'=4,'x'=4,'core'=2] {'z_hi'}, use_global_device_ids=true, to_apply=%region_2.0 | all-reduce | flops 2048 | bytes 16384 | tf_op jit(solution)/shard_map/psum | solution.py:256
  68.2 12.5 %all_to_all.26 = f32[32,8,256]{2,1,0:T(8,128)S(1)} all-to-all(f32[32,8,256]{2,1,0:T(8,128)S(1)} %broadcast_in_dim.4), channel_id=1, replica_groups=mesh['z_hi'=8,'z_lo'=4,'y'=4,'x'=4,'core'=2] {'y','x','core'}, dimensions={0} | all-to-all | bytes 524288 | tf_op jit(solution)/shard_map/all_to_all | solution.py:236
  80.8 0.0 copy-done
  80.8 9.1 %shard_map.42 = (f32[64,256]{1,0:T(8,128)}, f32[8,12,8,256]{3,2,1,0:T(8,128)S(1)}) custom-call(f32[256,256]{1,0:T(8,128)S(1)} %bitcast.7, f32[64,256]{1,0:T(8,128)S(1)} %bitcast.9, f32[12,256,256]{2,1,0:T(8,128)S(1)} %get-tuple-element.7.slab_ref), custom_call_target="tpu_custom_call" | custom-call | tf_op jit(solution)/shard_map/pallas_call | solution.py:187
  89.9 15.9 %all_to_all.27 = f32[8,12,8,256]{3,2,1,0:T(8,128)S(1)} all-to-all(f32[8,12,8,256]{3,2,1,0:T(8,128)S(1)} %get-tuple-element.9), channel_id=1, replica_groups=mesh['z_hi'=8,'z_lo'=4,'y'=4,'x'=4,'core'=2] {'x','core'}, dimensions={0} | all-to-all | bytes 1572864 | tf_op jit(solution)/shard_map/all_to_all | solution.py:236
  105.8 0.6 shard_map.43
  106.4 8.0 %all_to_all.28 = f32[8,12,96]{2,1,0:T(8,128)S(1)} all-to-all(f32[8,12,96]{2,1,0:T(8,128)S(1)} %shard_map.43), channel_id=1, replica_groups=mesh['z_hi'=8,'z_lo'=4,'y'=4,'x'=4,'core'=2] {'x','core'}, dimensions={0} | all-to-all | bytes 73728 | tf_op jit(solution)/shard_map/all_to_all | solution.py:236
  114.4 11.5 %all_to_all.29 = f32[16,12,96]{2,1,0:T(8,128)S(1)} all-to-all(f32[16,12,96]{2,1,0:T(8,128)S(1)} %broadcast_in_dim.5), channel_id=1, replica_groups=mesh['z_hi'=8,'z_lo'=4,'y'=4,'x'=4,'core'=2] {'z_lo','y'}, dimensions={0} | all-to-all | bytes 147456 | tf_op jit(solution)/shard_map/all_to_all | solution.py:236
  126.0 24.0 %psum.23 = f32[12,96]{1,0:T(8,128)} all-reduce(f32[12,96]{1,0:T(8,128)S(1)} %reduce_sum.29), channel_id=1, replica_groups=mesh['z_hi'=8,'z_lo'=4,'y'=4,'x'=4,'core'=2] {'z_hi'}, use_global_device_ids=true, to_apply=%region_5.0 | all-reduce | flops 1152 | bytes 9216 | tf_op jit(solution)/shard_map/psum | solution.py:264
  (5 shorter events, 0.1 us)
Async XLA Ops:
  0.6 80.1 %copy-start = (f32[256,64]{0,1:T(8,128)S(1)}, f32[256,64]{0,1:T(8,128)}, u32[]{:S(2)}) copy-start(f32[256,64]{0,1:T(8,128)} %param.3) | copy-start | bytes 196612

commit v5 on v4

--- a/solution.py
+++ b/solution.py
@@ -132,35 +132,35 @@
     )
 
 
-def orthonormalize(columns):
+def orthonormalize(rows):
     for factor in (inverse_factor, near_inverse_factor):
-        inner_gram = dot_full(columns, columns, ((0,), (0,)))
-        columns = dot_full(columns, factor(inner_gram), ((1,), (1,)))
-    return columns
+        inner_gram = dot_full(rows, rows, ((1,), (1,)))
+        rows = dot_full(factor(inner_gram), rows, ((1,), (0,)))
+    return rows
 
 
 def core_kernel(gram_ref, start_ref, slab_ref, subspace_ref, core_ref):
     gram = gram_ref[...]
-    subspace = start_ref[...].T
+    subspace = start_ref[...]
     for repeat in range(POWER):
-        subspace = orthonormalize(dot_full(gram, subspace, ((1,), (0,))))
-    subspace_ref[...] = subspace.T
+        subspace = orthonormalize(dot_full(subspace, gram, ((1,), (0,))))
+    subspace_ref[...] = subspace
     hours, cells, kpis = slab_ref.shape
-    keep = subspace.shape[1]
+    keep = subspace.shape[0]
     devices, _, group, width = core_ref.shape
     quarters = width // keep
     quarter = cells // quarters
     basis_high, basis_low = split(subspace)
-    plain = ((1,), (0,))
+    last = ((1,), (1,))
 
     def place(basis, q):
         parts = []
         if q:
-            parts.append(jnp.zeros((kpis, keep * q), BF16))
+            parts.append(jnp.zeros((keep * q, kpis), BF16))
         parts.append(basis)
         if q < quarters - 1:
-            parts.append(jnp.zeros((kpis, keep * (quarters - 1 - q)), BF16))
-        return jnp.concatenate(parts, axis=1)
+            parts.append(jnp.zeros((keep * (quarters - 1 - q), kpis), BF16))
+        return jnp.concatenate(parts, axis=0)
 
     bases = [(place(basis_high, q), place(basis_low, q)) for q in range(quarters)]
     batch = 4
@@ -169,9 +169,9 @@
         for q in range(quarters):
             at = pl.ds(q * quarter, quarter)
             top, rest = split(slab_ref[h : h + batch, at, :].reshape(batch * quarter, kpis))
-            total += dot(top, bases[q][0], plain)
-            total += dot(top, bases[q][1], plain)
-            total += dot(rest, bases[q][0], plain)
+            total += dot(top, bases[q][0], last)
+            total += dot(top, bases[q][1], last)
+            total += dot(rest, bases[q][0], last)
         for i in range(batch):
             for j in range(devices):
                 at = i * quarter + j * group

time: 150 us -> 149 us (level)
  Pallas kernels: 12.9 us -> 11.2 us
    pallas_call x1, Pallas kernels: 9.12 us -> 7.43 us  [subspace_and_core(): pl.pallas_call(core_kernel, in_specs=[vmem] * 3, out_specs=[vmem, vmem],...]
where the time goes in v5:
time: 149 us; the launch traced here: 148 us
  blocking collectives  136 us (91%)
  Pallas kernels  11.2 us (8%)
    all_to_all x5, blocking collectives, swap(): return lax.all_to_all(values, axes, 0, 0, tiled=True)  71.3 us
    psum x1, blocking collectives, local(): piece = lax.psum(lax.optimization_barrier(piece), 'z_hi')  32.5 us
    psum x1, blocking collectives, local(): hour_gram = lax.psum(rows, 'z_hi')  24 us
    psum x1, blocking collectives, local(): piece = lax.psum(jnp.sum(swap(pieces, NEAR), axis=0), 'z_lo')  8.55 us
    pallas_call x1, Pallas kernels, subspace_and_core(): pl.pallas_call(core_kernel, in_specs=[vmem] * 3, out_specs=[vmem, vmem],...  7.43 us
    pallas_call x1, Pallas kernels, slab_gram(): pl.pallas_call(functools.partial(gram_kernel, scale), in_specs=[pl.BlockS...  3.11 us

profile of v5, /device:TPU:8, one launch (start us, length us, event | category | flops | bytes accessed | tf_op | source)
XLA Modules:
  0.0 148.3 jit_solution(4731742111644147601)
XLA Ops:
  0.6 0.0 copy-start
  0.6 3.1 %shard_map.41 = (f32[256,256]{1,0:T(8,128)S(1)}, f32[12,256,256]{2,1,0:T(8,128)S(1)}) custom-call(f32[12,256,256]{2,1,0:T(8,128)} %bitcast.10), custom_call_target="tpu_custom_call" | custom-call | tf_op jit(solution)/shard_map/pallas_call | solution.py:57
  3.8 23.3 %all_to_all.25 = f32[32,8,256]{2,1,0:T(8,128)S(1)} all-to-all(f32[32,8,256]{2,1,0:T(8,128)S(1)} %bitcast.8), channel_id=1, replica_groups=mesh['z_hi'=8,'z_lo'=4,'y'=4,'x'=4,'core'=2] {'y','x','core'}, dimensions={0} | all-to-all | bytes 524288 | tf_op jit(solution)/shard_map/all_to_all | solution.py:236
  27.1 8.5 %psum.21 = f32[8,256]{1,0:T(8,128)S(1)} all-reduce(f32[8,256]{1,0:T(8,128)S(1)} %reduce_sum.27), channel_id=1, replica_groups=mesh['z_hi'=8,'z_lo'=4,'y'=4,'x'=4,'core'=2] {'z_lo'}, use_global_device_ids=true, to_apply=%region_1.0 | all-reduce | flops 2048 | bytes 16384 | tf_op jit(solution)/shard_map/psum | solution.py:255
  35.7 32.5 %psum.22 = f32[8,256]{1,0:T(8,128)S(1)} all-reduce(f32[8,256]{1,0:T(8,128)S(1)} %psum.21), channel_id=1, replica_groups=mesh['z_hi'=8,'z_lo'=4,'y'=4,'x'=4,'core'=2] {'z_hi'}, use_global_device_ids=true, to_apply=%region_2.0 | all-reduce | flops 2048 | bytes 16384 | tf_op jit(solution)/shard_map/psum | solution.py:256
  68.2 12.5 %all_to_all.26 = f32[32,8,256]{2,1,0:T(8,128)S(1)} all-to-all(f32[32,8,256]{2,1,0:T(8,128)S(1)} %broadcast_in_dim.4), channel_id=1, replica_groups=mesh['z_hi'=8,'z_lo'=4,'y'=4,'x'=4,'core'=2] {'y','x','core'}, dimensions={0} | all-to-all | bytes 524288 | tf_op jit(solution)/shard_map/all_to_all | solution.py:236
  80.8 0.0 copy-done
  80.8 7.4 %shard_map.42 = (f32[64,256]{1,0:T(8,128)}, f32[8,12,8,256]{3,2,1,0:T(8,128)S(1)}) custom-call(f32[256,256]{1,0:T(8,128)S(1)} %bitcast.7, f32[64,256]{1,0:T(8,128)S(1)} %bitcast.9, f32[12,256,256]{2,1,0:T(8,128)S(1)} %get-tuple-element.7.slab_ref), custom_call_target="tpu_custom_call" | custom-call | tf_op jit(solution)/shard_map/pallas_call | solution.py:187
  88.2 15.9 %all_to_all.27 = f32[8,12,8,256]{3,2,1,0:T(8,128)S(1)} all-to-all(f32[8,12,8,256]{3,2,1,0:T(8,128)S(1)} %get-tuple-element.9), channel_id=1, replica_groups=mesh['z_hi'=8,'z_lo'=4,'y'=4,'x'=4,'core'=2] {'x','core'}, dimensions={0} | all-to-all | bytes 1572864 | tf_op jit(solution)/shard_map/all_to_all | solution.py:236
  104.1 0.6 shard_map.43
  104.7 8.0 %all_to_all.28 = f32[8,12,96]{2,1,0:T(8,128)S(1)} all-to-all(f32[8,12,96]{2,1,0:T(8,128)S(1)} %shard_map.43), channel_id=1, replica_groups=mesh['z_hi'=8,'z_lo'=4,'y'=4,'x'=4,'core'=2] {'x','core'}, dimensions={0} | all-to-all | bytes 73728 | tf_op jit(solution)/shard_map/all_to_all | solution.py:236
  112.8 11.5 %all_to_all.29 = f32[16,12,96]{2,1,0:T(8,128)S(1)} all-to-all(f32[16,12,96]{2,1,0:T(8,128)S(1)} %broadcast_in_dim.5), channel_id=1, replica_groups=mesh['z_hi'=8,'z_lo'=4,'y'=4,'x'=4,'core'=2] {'z_lo','y'}, dimensions={0} | all-to-all | bytes 147456 | tf_op jit(solution)/shard_map/all_to_all | solution.py:236
  124.3 24.0 %psum.23 = f32[12,96]{1,0:T(8,128)} all-reduce(f32[12,96]{1,0:T(8,128)S(1)} %reduce_sum.29), channel_id=1, replica_groups=mesh['z_hi'=8,'z_lo'=4,'y'=4,'x'=4,'core'=2] {'z_hi'}, use_global_device_ids=true, to_apply=%region_5.0 | all-reduce | flops 1152 | bytes 9216 | tf_op jit(solution)/shard_map/psum | solution.py:264
  (5 shorter events, 0.1 us)
Async XLA Ops:
  0.6 80.1 %copy-start = (f32[256,64]{0,1:T(8,128)S(1)}, f32[256,64]{0,1:T(8,128)}, u32[]{:S(2)}) copy-start(f32[256,64]{0,1:T(8,128)} %param.3) | copy-start | bytes 196612

commit v6 on v5

--- a/solution.py
+++ b/solution.py
@@ -152,26 +152,31 @@
     quarter = cells // quarters
     basis_high, basis_low = split(subspace)
     last = ((1,), (1,))
-
-    def place(basis, q):
-        parts = []
-        if q:
-            parts.append(jnp.zeros((keep * q, kpis), BF16))
-        parts.append(basis)
-        if q < quarters - 1:
-            parts.append(jnp.zeros((keep * (quarters - 1 - q), kpis), BF16))
-        return jnp.concatenate(parts, axis=0)
-
-    bases = [(place(basis_high, q), place(basis_low, q)) for q in range(quarters)]
+    none = jnp.zeros((keep, kpis), BF16)
+    basis = jnp.concatenate(
+        [
+            jnp.concatenate(blocks, axis=1)
+            for blocks in (
+                (basis_high, none, basis_high, none),
+                (none, basis_high, none, basis_high),
+                (basis_low, none, none, none),
+                (none, basis_low, none, none),
+            )
+        ],
+        axis=0,
+    )
     batch = 4
     for h in range(0, hours, batch):
-        total = jnp.zeros((batch * quarter, width), F32)
-        for q in range(quarters):
-            at = pl.ds(q * quarter, quarter)
-            top, rest = split(slab_ref[h : h + batch, at, :].reshape(batch * quarter, kpis))
-            total += dot(top, bases[q][0], last)
-            total += dot(top, bases[q][1], last)
-            total += dot(rest, bases[q][0], last)
+        parts = []
+        for q in range(0, quarters, 2):
+            pair = []
+            for side in (q, q + 1):
+                at = pl.ds(side * quarter, quarter)
+                pair.append(split(slab_ref[h : h + batch, at, :].reshape(batch * quarter, kpis)))
+            columns = jnp.concatenate([pair[0][0], pair[1][0], pair[0][1], pair[1][1]], axis=1)
+            both = dot(columns, basis, last)
+            parts.append(both[:, : 2 * keep] + both[:, 2 * keep :])
+        total = jnp.concatenate(parts, axis=1)
         for i in range(batch):
             for j in range(devices):
                 at = i * quarter + j * group

time: 149 us -> 148 us (level)
  no operation moved by 1% of the time
where the time goes in v6:
time: 148 us
  blocking collectives  136 us (92%)
  Pallas kernels  10.8 us (7%)
    all_to_all x5, blocking collectives, swap(): return lax.all_to_all(values, axes, 0, 0, tiled=True)  71.2 us
    psum x1, blocking collectives, local(): piece = lax.psum(lax.optimization_barrier(piece), 'z_hi')  32.5 us
    psum x1, blocking collectives, local(): hour_gram = lax.psum(rows, 'z_hi')  24.2 us
    psum x1, blocking collectives, local(): piece = lax.psum(jnp.sum(swap(pieces, NEAR), axis=0), 'z_lo')  8.55 us
    pallas_call x1, Pallas kernels, subspace_and_core(): pl.pallas_call(core_kernel, in_specs=[vmem] * 3, out_specs=[vmem, vmem],...  7.06 us
    pallas_call x1, Pallas kernels, slab_gram(): pl.pallas_call(functools.partial(gram_kernel, scale), in_specs=[pl.BlockS...  3.11 us

profile of v6, /device:TPU:8, one launch (start us, length us, event | category | flops | bytes accessed | tf_op | source)
XLA Modules:
  0.0 148.1 jit_solution(9723121060197710563)
XLA Ops:
  0.6 0.0 copy-start
  0.6 3.1 %shard_map.41 = (f32[256,256]{1,0:T(8,128)S(1)}, f32[12,256,256]{2,1,0:T(8,128)S(1)}) custom-call(f32[12,256,256]{2,1,0:T(8,128)} %bitcast.10), custom_call_target="tpu_custom_call" | custom-call | tf_op jit(solution)/shard_map/pallas_call | solution.py:57
  3.8 23.3 %all_to_all.25 = f32[32,8,256]{2,1,0:T(8,128)S(1)} all-to-all(f32[32,8,256]{2,1,0:T(8,128)S(1)} %bitcast.8), channel_id=1, replica_groups=mesh['z_hi'=8,'z_lo'=4,'y'=4,'x'=4,'core'=2] {'y','x','core'}, dimensions={0} | all-to-all | bytes 524288 | tf_op jit(solution)/shard_map/all_to_all | solution.py:241
  27.1 8.5 %psum.21 = f32[8,256]{1,0:T(8,128)S(1)} all-reduce(f32[8,256]{1,0:T(8,128)S(1)} %reduce_sum.27), channel_id=1, replica_groups=mesh['z_hi'=8,'z_lo'=4,'y'=4,'x'=4,'core'=2] {'z_lo'}, use_global_device_ids=true, to_apply=%region_1.0 | all-reduce | flops 2048 | bytes 16384 | tf_op jit(solution)/shard_map/psum | solution.py:260
  35.7 32.5 %psum.22 = f32[8,256]{1,0:T(8,128)S(1)} all-reduce(f32[8,256]{1,0:T(8,128)S(1)} %psum.21), channel_id=1, replica_groups=mesh['z_hi'=8,'z_lo'=4,'y'=4,'x'=4,'core'=2] {'z_hi'}, use_global_device_ids=true, to_apply=%region_2.0 | all-reduce | flops 2048 | bytes 16384 | tf_op jit(solution)/shard_map/psum | solution.py:261
  68.2 12.5 %all_to_all.26 = f32[32,8,256]{2,1,0:T(8,128)S(1)} all-to-all(f32[32,8,256]{2,1,0:T(8,128)S(1)} %broadcast_in_dim.4), channel_id=1, replica_groups=mesh['z_hi'=8,'z_lo'=4,'y'=4,'x'=4,'core'=2] {'y','x','core'}, dimensions={0} | all-to-all | bytes 524288 | tf_op jit(solution)/shard_map/all_to_all | solution.py:241
  80.8 0.0 copy-done
  80.8 7.1 %shard_map.42 = (f32[64,256]{1,0:T(8,128)}, f32[8,12,8,256]{3,2,1,0:T(8,128)S(1)}) custom-call(f32[256,256]{1,0:T(8,128)S(1)} %bitcast.7, f32[64,256]{1,0:T(8,128)S(1)} %bitcast.9, f32[12,256,256]{2,1,0:T(8,128)S(1)} %get-tuple-element.7.slab_ref), custom_call_target="tpu_custom_call" | custom-call | tf_op jit(solution)/shard_map/pallas_call | solution.py:192
  87.8 15.9 %all_to_all.27 = f32[8,12,8,256]{3,2,1,0:T(8,128)S(1)} all-to-all(f32[8,12,8,256]{3,2,1,0:T(8,128)S(1)} %get-tuple-element.9), channel_id=1, replica_groups=mesh['z_hi'=8,'z_lo'=4,'y'=4,'x'=4,'core'=2] {'x','core'}, dimensions={0} | all-to-all | bytes 1572864 | tf_op jit(solution)/shard_map/all_to_all | solution.py:241
  103.7 0.6 shard_map.43
  104.4 8.0 %all_to_all.28 = f32[8,12,96]{2,1,0:T(8,128)S(1)} all-to-all(f32[8,12,96]{2,1,0:T(8,128)S(1)} %shard_map.43), channel_id=1, replica_groups=mesh['z_hi'=8,'z_lo'=4,'y'=4,'x'=4,'core'=2] {'x','core'}, dimensions={0} | all-to-all | bytes 73728 | tf_op jit(solution)/shard_map/all_to_all | solution.py:241
  112.4 11.5 %all_to_all.29 = f32[16,12,96]{2,1,0:T(8,128)S(1)} all-to-all(f32[16,12,96]{2,1,0:T(8,128)S(1)} %broadcast_in_dim.5), channel_id=1, replica_groups=mesh['z_hi'=8,'z_lo'=4,'y'=4,'x'=4,'core'=2] {'z_lo','y'}, dimensions={0} | all-to-all | bytes 147456 | tf_op jit(solution)/shard_map/all_to_all | solution.py:241
  123.9 24.2 %psum.23 = f32[12,96]{1,0:T(8,128)} all-reduce(f32[12,96]{1,0:T(8,128)S(1)} %reduce_sum.29), channel_id=1, replica_groups=mesh['z_hi'=8,'z_lo'=4,'y'=4,'x'=4,'core'=2] {'z_hi'}, use_global_device_ids=true, to_apply=%region_5.0 | all-reduce | flops 1152 | bytes 9216 | tf_op jit(solution)/shard_map/psum | solution.py:269
  (5 shorter events, 0.1 us)
Async XLA Ops:
  0.6 80.1 %copy-start = (f32[256,64]{0,1:T(8,128)S(1)}, f32[256,64]{0,1:T(8,128)}, u32[]{:S(2)}) copy-start(f32[256,64]{0,1:T(8,128)} %param.3) | copy-start | bytes 196612
